TPU v7x, 512 devices: a whole 4x8x8 slice. The times are simulated.
512 devices in a mesh: lon: 32 (over x, z_hi, core), lat: 16 (over y, z_lo).
Axes of the slice: x: 4, y: 8, z: 8 (z_hi: 4, z_lo: 2; z = z_hi * 2 + z_lo), core: 2. Of those that a mesh axis runs over, the one named last changes fastest.
Arguments:
- fields: bfloat16 [1, 64, 256, 4096], P(None, None, 'lat', 'lon'), may hold values from -6 to 6
- cotangent: bfloat16 [1, 64, 256, 4096], P(None, None, 'lat', 'lon'), may hold values from -6 to 6
- ocean_mask: int32 [256, 4096], P('lat', 'lon'), may hold values 0 or 1
- seam_partner: int32 [4096], replicated, may hold values from 0 to 4095, as said below
- depth_weight: bfloat16 [64, 7, 7], replicated, may hold values from -0.875 to 0.875
- norm_gain: bfloat16 [64], replicated, may hold values from 0.5 to 1.5
- layer_norm_bias: bfloat16 [64], replicated, may hold values from -3 to 3
- up_weight: bfloat16 [256, 64], replicated, may hold values from -0.75 to 0.75
- up_bias: bfloat16 [256], replicated, may hold values from -3 to 3
- down_weight: bfloat16 [64, 256], replicated, may hold values from -0.375 to 0.375
- layer_scale: bfloat16 [64], replicated, may hold values from 0.5 to 1.5
Outputs:
- output: bfloat16 [1, 64, 256, 4096], P(None, None, 'lat', 'lon')
- grad_fields: bfloat16 [1, 64, 256, 4096], P(None, None, 'lat', 'lon')
- grad_depth: float32 [64, 7, 7], replicated
- grad_gain: float32 [64], replicated
- grad_bias: float32 [64], replicated
- grad_up_weight: float32 [256, 64], replicated
- grad_up_bias: float32 [256], replicated
- grad_down_weight: float32 [64, 256], replicated
- grad_scale: float32 [64], replicated
Inputs may be any that keep to these rules, and one draw needn't show every extreme that they name: seam_partner[i] = (s - i) mod 4096 for one whole number s, so it is its own inverse.
All inputs are finite; a program needn't handle non-finite values. No bound on the sum of `ocean_mask` on one device may be relied on, other than what follows from the above.
Results may differ from a plain program's by a relative error of at most 0.0068.
Values may be sent and summed in bfloat16 or wider, within the bound.
A program may use at most 64 MiB of HBM per device.

v0:
```python
import math
import jax
import jax.numpy as jnp
from jax import lax
from jax.sharding import PartitionSpec as P


def extended_2(cells, sides, width, closed):
    for axis, dim in sides:
        count = lax.axis_size(axis)
        ends = count if closed else count - 1
        head = lax.slice_in_dim(cells, 0, width, axis=dim)
        tail = lax.slice_in_dim(cells, cells.shape[dim] - width, cells.shape[dim], axis=dim)
        cells = jnp.concatenate(
            [
                lax.ppermute(tail, axis, [(i, (i + 1) % count) for i in range(ends)]),
                cells,
                lax.ppermute(head, axis, [((i + 1) % count, i) for i in range(ends)]),
            ],
            axis=dim,
        )
    return cells


def gelu_slope(pre):
    cdf = 0.5 * (1.0 + lax.erf(pre / math.sqrt(2.0)))
    return cdf + pre * jnp.exp(-0.5 * pre * pre) / math.sqrt(2.0 * math.pi)


def cell_terms(
    conv, field, cot, mask, norm_gain, layer_norm_bias, up_weight, up_bias, down_weight, layer_scale
):
    mean_c = jnp.mean(conv, axis=0, keepdims=True)
    centered_input = conv - mean_c
    var_c = jnp.mean(centered_input * centered_input, axis=0, keepdims=True)
    reciprocal_deviation = lax.rsqrt(var_c + 1e-06)
    standardized_input = centered_input * reciprocal_deviation
    layer_norm_gain = norm_gain.astype(jnp.float32)[:, None]
    normalized_output = (
        standardized_input * layer_norm_gain + layer_norm_bias.astype(jnp.float32)[:, None]
    ).astype(jnp.bfloat16)
    pre = (
        jnp.dot(up_weight, normalized_output, preferred_element_type=jnp.float32)
        + up_bias.astype(jnp.float32)[:, None]
    )
    hidden = jax.nn.gelu(pre, approximate=False).astype(jnp.bfloat16)
    branch = jnp.dot(down_weight, hidden, preferred_element_type=jnp.float32)
    scale = layer_scale.astype(jnp.float32)[:, None]
    out = (mask * (field.astype(jnp.float32) + scale * branch)).astype(jnp.bfloat16)
    grad_in = mask * cot.astype(jnp.float32)
    d_branch = (grad_in * scale).astype(jnp.bfloat16)
    g_scale = jnp.sum(grad_in * branch, axis=1)
    contract_cells = (((1,), (1,)), ((), ()))
    contract_first = (((0,), (0,)), ((), ()))
    g_down = lax.dot_general(d_branch, hidden, contract_cells, preferred_element_type=jnp.float32)
    d_hidden = lax.dot_general(
        down_weight, d_branch, contract_first, preferred_element_type=jnp.float32
    )
    d_pre = (d_hidden * gelu_slope(pre)).astype(jnp.bfloat16)
    g_up_b = jnp.sum(d_pre.astype(jnp.float32), axis=1)
    g_up_w = lax.dot_general(
        d_pre, normalized_output, contract_cells, preferred_element_type=jnp.float32
    )
    normalized_gradient = lax.dot_general(
        up_weight, d_pre, contract_first, preferred_element_type=jnp.float32
    )
    gain_gradient = jnp.sum(normalized_gradient * standardized_input, axis=1)
    g_bias = jnp.sum(normalized_gradient, axis=1)
    gradient_through_norm = normalized_gradient * layer_norm_gain
    convolution_gradient = reciprocal_deviation * (
        gradient_through_norm
        - jnp.mean(gradient_through_norm, axis=0, keepdims=True)
        - standardized_input
        * jnp.mean(gradient_through_norm * standardized_input, axis=0, keepdims=True)
    )
    return (
        out,
        convolution_gradient.astype(jnp.bfloat16),
        (gain_gradient, g_bias, g_up_w, g_up_b, g_down, g_scale),
    )


def make_picker(wanted, carry, piece):
    width = piece.shape[3]
    inside = (wanted >= 0) & (wanted < width)
    picked = jnp.take(piece, jnp.clip(wanted, 0, width - 1), axis=3)
    return jnp.where(inside[None, None, None, :], picked, carry)


def shards(
    fields,
    cotangent,
    ocean_mask,
    seam_partner,
    depth_weight,
    norm_gain,
    layer_norm_bias,
    up_weight,
    up_bias,
    down_weight,
    layer_scale,
):
    samples, chans, rows, cols = fields.shape
    total_lon = seam_partner.shape[0]
    lon_start = lax.axis_index("lon") * cols
    positions = (lon_start + jnp.arange(-3, cols + 3, dtype=jnp.int32)) % total_lon
    partner_cols = jnp.take(seam_partner, positions)
    own_partner = partner_cols[3 : cols + 3]
    is_top = lax.axis_index("lat") == lax.axis_size("lat") - 1
    weight_f = depth_weight.astype(jnp.float32)
    mask_f = ocean_mask.astype(jnp.float32)
    lon_padded = extended_2(fields, (("lon", 3),), 3, True)
    banded = extended_2(lon_padded, (("lat", 2),), 3, False)
    upper = fields[:, :, rows - 3 :, :][:, :, ::-1, :]
    fold_init = jnp.zeros((samples, chans, 3, cols + 6), jnp.bfloat16)
    folded = make_picker(partner_cols, fold_init, lax.all_gather(upper, "lon", axis=3, tiled=True))
    top_rows = jnp.where(is_top, folded, banded[:, :, rows + 3 :, :])
    extended = jnp.concatenate([banded[:, :, : rows + 3, :], top_rows], axis=2)
    conv = jnp.zeros((samples, chans, rows, cols), jnp.float32)
    for row_tap in range(7):
        for col_tap in range(7):
            conv = conv + weight_f[:, row_tap, col_tap][None, :, None, None] * extended[
                :, :, row_tap : row_tap + rows, col_tap : col_tap + cols
            ].astype(jnp.float32)
    mask_flat = mask_f.reshape(1, rows * cols)
    out_s, dconv_s, parts = cell_terms(
        conv[0].reshape(chans, rows * cols),
        fields[0].reshape(chans, rows * cols),
        cotangent[0].reshape(chans, rows * cols),
        mask_flat,
        norm_gain,
        layer_norm_bias,
        up_weight,
        up_bias,
        down_weight,
        layer_scale,
    )
    outputs = [out_s.reshape(chans, rows, cols)]
    dconv_list = [dconv_s.reshape(chans, rows, cols)]
    output = jnp.stack(outputs)
    convolution_gradient = jnp.stack(dconv_list)
    d_conv_f = convolution_gradient.astype(jnp.float32)
    taps = []
    for row_tap in range(7):
        line = []
        for col_tap in range(7):
            line.append(
                jnp.sum(
                    d_conv_f
                    * extended[:, :, row_tap : row_tap + rows, col_tap : col_tap + cols].astype(
                        jnp.float32
                    ),
                    axis=(0, 2, 3),
                )
            )
        taps.append(jnp.stack(line, axis=1))
    g_depth = jnp.stack(taps, axis=1)
    lon_back = extended_2(convolution_gradient, (("lon", 3),), 3, True)
    band_back = extended_2(lon_back, (("lat", 2),), 3, False)
    deeper = jnp.pad(band_back, ((0, 0), (0, 0), (0, 3), (0, 0)))
    spread = jnp.zeros((samples, chans, rows + 3, cols), jnp.float32)
    for row_tap in range(7):
        for col_tap in range(7):
            spread = spread + weight_f[:, row_tap, col_tap][None, :, None, None] * deeper[
                :, :, 6 - row_tap : 9 - row_tap + rows, 6 - col_tap : 6 - col_tap + cols
            ].astype(jnp.float32)
    own = spread[:, :, :rows, :]
    margin = spread[:, :, rows:, :]
    back_init = jnp.zeros((samples, chans, 3, cols), jnp.float32)
    back = make_picker(
        own_partner,
        back_init,
        lax.all_gather(margin.astype(jnp.bfloat16), "lon", axis=3, tiled=True).astype(jnp.float32),
    )
    extra = back[:, :, ::-1, :]
    own = own.at[:, :, rows - 3 :, :].add(jnp.where(is_top, extra, 0.0))
    grad_fields = (mask_f[None, None] * cotangent.astype(jnp.float32) + own).astype(jnp.bfloat16)
    gain_gradient, g_bias, g_up_w, g_up_b, g_down, g_scale = parts
    summed = lax.psum(
        (g_depth, gain_gradient, g_bias, g_up_w, g_up_b, g_down, g_scale), ("lon", "lat")
    )
    return (
        output,
        grad_fields,
        summed[0],
        summed[1],
        summed[2],
        summed[3],
        summed[4],
        summed[5],
        summed[6],
    )


def solution(mesh):
    placed = (
        P(None, None, "lat", "lon"),
        P(None, None, "lat", "lon"),
        P("lat", "lon"),
        P(),
        P(),
        P(),
        P(),
        P(),
        P(),
        P(),
        P(),
    )
    return jax.shard_map(
        shards,
        mesh=mesh,
        in_specs=placed,
        out_specs=(
            P(None, None, "lat", "lon"),
            P(None, None, "lat", "lon"),
            P(),
            P(),
            P(),
            P(),
            P(),
            P(),
            P(),
        ),
        check_vma=False,
    )
```

profile of v0, /device:TPU:1, one launch (start us, length us, event | category | flops | bytes accessed | tf_op | source)
XLA Modules:
  0.0 497.8 jit_solution(14033838073368291433)
XLA Ops:
  7.3 1.0 slice.730
  9.0 1.5 copy.94
  10.5 7.2 %collective-permute-start = (bf16[1,64,16,3]{1,2,3,0:T(8,128)(2,1)S(1)}, bf16[1,64,16,3]{1,2,3,0:T(8,128)(2,1)S(1)}, u32[]{:S(2)}, u32[]{:S(2)}) collective-permute-start(bf16[1,64,16,3]{1,2,3,0:T(8,128)(2,1)S(1)} %get-tuple-element.147), channel_id=1, source_target_pairs={{0,16},{16,32},{32,48},{48,64},{64,80},{80,96},{96,112},{112,128},... | collective-permute-start | bytes 18440 | tf_op jit(solution)/shard_map/ppermute | solution.py:16
  17.7 3.5 collective-permute-start.1
  22.0 2.0 gather_fusion
  27.0 1.3 collective-permute-start.3
  28.9 1.4 copy.95
  31.9 1.1 copy.108
  33.5 4.2 collective-permute-start.2
  37.7 42.1 %all-gather.3.cloned.1.call-done = bf16[1,64,3,4096]{3,1,2,0:T(8,128)(2,1)} async-done(((bf16[1,64,3,128]{3,1,2,0:T(8,128)(2,1)}), bf16[1,64,3,4096]{3,1,2,0:T(8,128)(2,1)}) %all-gather.3.cloned.1.call-update) | async-done | bytes 1572880 | tf_op jit(solution)/shard_map/all_gather | solution.py:116
  79.8 6.4 %copy.102 = bf16[1,64,3,4096]{1,2,3,0:T(4,128)(2,1)} copy(bf16[1,64,3,4096]{3,1,2,0:T(8,128)(2,1)} %all-gather.3.cloned.1.call-done) | data formatting | bytes 3145728 | tf_op jit(solution)/shard_map/all_gather | solution.py:116
  86.2 3.0 gather_fusion.1
  90.4 10.0 %fusion.134 = (f32[16,128]{0,1:T(8,128)S(1)}, f32[1,64,16,128]{1,2,3,0:T(8,128)S(1)}) fusion(bf16[1,64,19,134]{1,2,3,0:T(8,128)(2,1)S(1)} %get-tuple-element.142, f32[64]{0:T(128)S(1)} %get-tuple-element.152, f32[64]{0:T(128)S(1)} %get-tuple-element.153, f32[64]{0:T(128)S(1)} %get-tuple-element.154, f32[64]{0:T(128)S(1)} %get-tuple-element.155, ...), kind=kLoop, calls=%fused_computation.375 | loop fusion | flops 20051968 | bytes 11829504 | tf_op jit(solution)/shard_map/reduce_sum | solution.py:33
  100.4 1.3 copy.103
  102.8 6.9 %fusion.5 = (bf16[256,2048]{0,1:T(8,128)(2,1)}, f32[256,2048]{0,1:T(8,128)S(1)}) fusion(f32[256]{0:T(256)S(1)} %copy-done.99, bf16[256,64]{0,1:T(8,128)(2,1)S(1)} %copy-done, f32[64]{0:T(128)S(1)} %copy-done.94, f32[64]{0:T(128)S(1)} %copy-done.85, f32[2048]{0:T(1024)S(1)} %rsqrt_bitcast_fusion, f32[2048]{0:T(1024)S(1)} %get-tuple-element.202, ...), kind=kOutput, calls=%fused_computation.63 | convolution fusion | flops 102367232 | bytes 3720704 | tf_op jit(solution)/shard_map/dot_general | solution.py:43
  109.7 2.0 convert_reduce_fusion
  111.7 1.1 fusion.121
  114.9 1.0 copy.109
  115.9 4.1 fusion.113
  120.2 3.2 collective-permute-start.4
  123.4 2.1 collective-permute-start.5
  125.5 1.6 fusion.112
  127.1 7.3 %collective-permute-done.5 = bf16[1,64,16,3]{3,1,2,0:T(8,128)(2,1)S(1)} collective-permute-done((bf16[1,64,16,3]{3,1,2,0:T(8,128)(2,1)S(1)}, bf16[1,64,16,3]{3,1,2,0:T(8,128)(2,1)S(1)}, u32[]{:S(2)}, u32[]{:S(2)}) %collective-permute-start.5) | collective-permute-done | bytes 6176 | tf_op jit(solution)/shard_map/ppermute | solution.py:18
  134.4 0.8 pad_maximum_fusion.8
  135.2 1.9 collective-permute-start.6
  137.2 1.3 collective-permute-start.7
  138.5 1.2 multiply_reduce_fusion.1
  140.3 0.7 copy.119
  141.3 1.3 stack.253
  142.6 1.3 stack.244
  143.9 1.3 stack.235
  145.2 1.4 pad_maximum_fusion.1
  146.7 1.8 pad_maximum_fusion.2
  148.7 6.7 %multiply_add_fusion = f32[1,64,19,128]{3,1,2,0:T(8,128)S(1)} fusion(bf16[1,64,19,134]{3,1,2,0:T(8,128)(2,1)S(1)} %get-tuple-element.138, bf16[1,64,22,134]{3,1,2,0:T(8,128)(2,1)S(1)} %pad_maximum_fusion.1, bf16[1,64,19,134]{3,1,2,0:T(8,128)(2,1)S(1)} %get-tuple-element.137, f32[64]{0:T(128)S(1)} %copy-done.53, f32[64]{0:T(128)S(1)} %copy-done.55, ...), kind=kLoop, calls=%fused_computation.239 | loop fusion | flops 22724608 | bytes 10078720 | tf_op jit(solution)/shard_map/add | solution.py:164
  155.4 0.9 copy-done.10
  157.0 1.2 fusion.92
  158.3 3.9 fusion.85
  162.2 0.7 stack.217
  164.5 1.7 fusion.132
  166.1 2.3 fusion.133
  168.5 107.1 %all-reduce.1 = (f32[64,7,7]{0,2,1:T(8,128)}, f32[64]{0:T(128)}, f32[64]{0:T(128)}, f32[256]{0:T(256)}, f32[64]{0:T(128)}) all-reduce(f32[64,7,7]{0,2,1:T(8,128)S(1)} %constant_dynamic-update-slice_fusion, f32[64]{0:T(128)S(1)} %copy-done.92, f32[64]{0:T(128)S(1)} %copy-done.91, ...), channel_id=1, replica_groups=mesh['lon'=32,'lat'=16] {'lon','lat'}, use_global_device_ids=true, to_apply=%region_53.54 | all-reduce | flops 3584 | bytes 28672 | tf_op jit(solution)/shard_map/psum | solution.py:179
  275.6 6.4 %copy.112 = bf16[1,64,3,4096]{1,2,3,0:T(4,128)(2,1)} copy(bf16[1,64,3,4096]{3,1,2,0:T(8,128)(2,1)} %all-gather.5.cloned.1.call-done) | data formatting | bytes 3145728 | tf_op jit(solution)/shard_map/all_gather | solution.py:173
  282.1 6.3 %bitcast_convert_fusion = f32[64,3,4096]{0,1,2:T(4,128)} fusion(bf16[1,64,3,4096]{1,2,3,0:T(4,128)(2,1)} %copy.112), kind=kLoop, calls=%fused_computation.52 | loop fusion | flops 786432 | bytes 4718592 | tf_op jit(solution)/shard_map/convert_element_type | solution.py:173
  288.3 4.3 gather_fusion.2
  292.9 0.9 copy.115
  293.8 194.5 %all-reduce.5.cloned.1.call-done = (f32[256,64]{0,1:T(8,128)}, f32[64,256]{1,0:T(8,128)}) async-done(((f32[256,64]{0,1:T(8,128)}, f32[64,256]{1,0:T(8,128)}), (f32[256,64]{0,1:T(8,128)}, f32[64,256]{1,0:T(8,128)})) %all-reduce.5.cloned.1.call-update) | async-done | bytes 131088 | tf_op jit(solution)/shard_map/psum | solution.py:179
  488.3 1.5 copy.159
  489.8 1.5 copy.160
  (266 shorter events, 14.3 us)
Async XLA Ops:
  7.2 95.5 %copy-start = (bf16[256,64]{0,1:T(8,128)(2,1)S(1)}, bf16[256,64]{0,1:T(8,128)(2,1)}, u32[]{:S(2)}) copy-start(bf16[256,64]{0,1:T(8,128)(2,1)} %param.20) | copy-start | bytes 98308
  7.2 19.0 %copy-start.27 = (s32[16,128]{1,0:T(8,128)S(1)}, s32[16,128]{1,0:T(8,128)}, u32[]{:S(2)}) copy-start(s32[16,128]{1,0:T(8,128)} %param.15) | copy-start | bytes 24580
  7.2 19.6 %copy-start.16 = (bf16[1,64,16,128]{3,2,1,0:T(8,128)(2,1)S(1)}, bf16[1,64,16,128]{3,2,1,0:T(8,128)(2,1)}, u32[]{:S(2)}) copy-start(bf16[1,64,16,128]{3,2,1,0:T(8,128)(2,1)} %param.14) | copy-start | bytes 786436
  7.2 72.6 %all-gather.3.cloned.1.call-start = ((), (), s32[]{:S(2)}) async-start(), calls=%async_computation | async-start | bytes 1622016 | tf_op jit(solution)/shard_map/all_gather | solution.py:116
  8.9 266.7 %all-gather.5.cloned.1.call-start = ((), (), s32[]{:S(2)}) async-start(), calls=%async_computation.1 | async-start | bytes 1622016 | tf_op jit(solution)/shard_map/all_gather | solution.py:173
  10.5 19.8 %copy-start.95 = (bf16[64]{0:T(256)(128)(2,1)S(1)}, bf16[64]{0:T(256)(128)(2,1)}, u32[]{:S(2)}) copy-start(bf16[64]{0:T(256)(128)(2,1)} %param.18) | copy-start | bytes 388
  10.5 20.3 %copy-start.96 = (bf16[64]{0:T(256)(128)(2,1)S(1)}, bf16[64]{0:T(256)(128)(2,1)}, u32[]{:S(2)}) copy-start(bf16[64]{0:T(256)(128)(2,1)} %param.19) | copy-start | bytes 388
  10.5 20.8 %copy-start.97 = (bf16[256]{0:T(256)(128)(2,1)S(1)}, bf16[256]{0:T(256)(128)(2,1)}, u32[]{:S(2)}) copy-start(bf16[256]{0:T(256)(128)(2,1)} %param.21) | copy-start | bytes 1540
  10.5 16.3 %collective-permute-start = (bf16[1,64,16,3]{1,2,3,0:T(8,128)(2,1)S(1)}, bf16[1,64,16,3]{1,2,3,0:T(8,128)(2,1)S(1)}, u32[]{:S(2)}, u32[]{:S(2)}) collective-permute-start(bf16[1,64,16,3]{1,2,3,0:T(8,128)(2,1)S(1)} %get-tuple-element.147), channel_id=1, source_target_pairs={{0,16},{16,32},{32,48},{48,64},{64,80},{80,96},{96,112},{112,128},... | collective-permute-start | bytes 18440 | tf_op jit(solution)/shard_map/ppermute | solution.py:16
  17.7 9.1 %collective-permute-start.1 = (bf16[1,64,16,3]{1,2,3,0:T(8,128)(2,1)S(1)}, bf16[1,64,16,3]{1,2,3,0:T(8,128)(2,1)S(1)}, u32[]{:S(2)}, u32[]{:S(2)}) collective-permute-start(bf16[1,64,16,3]{1,2,3,0:T(8,128)(2,1)S(1)} %get-tuple-element.148), channel_id=1, source_target_pairs={{16,0},{32,16},{48,32},{64,48},{80,64},{96,80},{112,96},{128,112},... | collective-permute-start | bytes 18440 | tf_op jit(solution)/shard_map/ppermute | solution.py:18
  24.7 65.4 %copy-start.28 = (f32[64]{0:T(128)}, f32[64]{0:T(128)S(1)}, u32[]{:S(2)}) copy-start(f32[64]{0:T(128)S(1)} %get-tuple-element.189) | copy-start | bytes 772
  24.7 65.4 %copy-start.30 = (f32[64]{0:T(128)}, f32[64]{0:T(128)S(1)}, u32[]{:S(2)}) copy-start(f32[64]{0:T(128)S(1)} %get-tuple-element.190) | copy-start | bytes 772
  24.7 65.4 %copy-start.32 = (f32[64]{0:T(128)}, f32[64]{0:T(128)S(1)}, u32[]{:S(2)}) copy-start(f32[64]{0:T(128)S(1)} %get-tuple-element.191) | copy-start | bytes 772
  24.7 65.4 %copy-start.34 = (f32[64]{0:T(128)}, f32[64]{0:T(128)S(1)}, u32[]{:S(2)}) copy-start(f32[64]{0:T(128)S(1)} %get-tuple-element.192) | copy-start | bytes 772
  24.7 65.4 %copy-start.36 = (f32[64]{0:T(128)}, f32[64]{0:T(128)S(1)}, u32[]{:S(2)}) copy-start(f32[64]{0:T(128)S(1)} %get-tuple-element.193) | copy-start | bytes 772
  24.7 65.4 %copy-start.38 = (f32[64]{0:T(128)}, f32[64]{0:T(128)S(1)}, u32[]{:S(2)}) copy-start(f32[64]{0:T(128)S(1)} %get-tuple-element.194) | copy-start | bytes 772
  24.7 65.4 %copy-start.40 = (f32[64]{0:T(128)}, f32[64]{0:T(128)S(1)}, u32[]{:S(2)}) copy-start(f32[64]{0:T(128)S(1)} %get-tuple-element.195) | copy-start | bytes 772
  24.8 65.4 %copy-start.42 = (f32[64]{0:T(128)}, f32[64]{0:T(128)S(1)}, u32[]{:S(2)}) copy-start(f32[64]{0:T(128)S(1)} %get-tuple-element.196) | copy-start | bytes 772
  24.8 65.4 %copy-start.44 = (f32[64]{0:T(128)}, f32[64]{0:T(128)S(1)}, u32[]{:S(2)}) copy-start(f32[64]{0:T(128)S(1)} %get-tuple-element.197) | copy-start | bytes 772
  24.8 65.4 %copy-start.46 = (f32[64]{0:T(128)}, f32[64]{0:T(128)S(1)}, u32[]{:S(2)}) copy-start(f32[64]{0:T(128)S(1)} %get-tuple-element.198) | copy-start | bytes 772
  24.8 65.4 %copy-start.48 = (f32[64]{0:T(128)}, f32[64]{0:T(128)S(1)}, u32[]{:S(2)}) copy-start(f32[64]{0:T(128)S(1)} %get-tuple-element.199) | copy-start | bytes 772
  25.4 64.8 %copy-start.50 = (f32[64]{0:T(128)}, f32[64]{0:T(128)S(1)}, u32[]{:S(2)}) copy-start(f32[64]{0:T(128)S(1)} %get-tuple-element.151) | copy-start | bytes 772
  25.4 64.8 %copy-start.52 = (f32[64]{0:T(128)}, f32[64]{0:T(128)S(1)}, u32[]{:S(2)}) copy-start(f32[64]{0:T(128)S(1)} %get-tuple-element.152) | copy-start | bytes 772
  25.4 64.8 %copy-start.54 = (f32[64]{0:T(128)}, f32[64]{0:T(128)S(1)}, u32[]{:S(2)}) copy-start(f32[64]{0:T(128)S(1)} %get-tuple-element.153) | copy-start | bytes 772
  25.4 64.8 %copy-start.56 = (f32[64]{0:T(128)}, f32[64]{0:T(128)S(1)}, u32[]{:S(2)}) copy-start(f32[64]{0:T(128)S(1)} %get-tuple-element.154) | copy-start | bytes 772
  25.4 64.8 %copy-start.58 = (f32[64]{0:T(128)}, f32[64]{0:T(128)S(1)}, u32[]{:S(2)}) copy-start(f32[64]{0:T(128)S(1)} %get-tuple-element.155) | copy-start | bytes 772
  25.4 64.8 %copy-start.60 = (f32[64]{0:T(128)}, f32[64]{0:T(128)S(1)}, u32[]{:S(2)}) copy-start(f32[64]{0:T(128)S(1)} %get-tuple-element.156) | copy-start | bytes 772
  25.4 64.8 %copy-start.62 = (f32[64]{0:T(128)}, f32[64]{0:T(128)S(1)}, u32[]{:S(2)}) copy-start(f32[64]{0:T(128)S(1)} %get-tuple-element.157) | copy-start | bytes 772
  25.5 64.8 %copy-start.64 = (f32[64]{0:T(128)}, f32[64]{0:T(128)S(1)}, u32[]{:S(2)}) copy-start(f32[64]{0:T(128)S(1)} %get-tuple-element.158) | copy-start | bytes 772
  25.5 64.8 %copy-start.66 = (f32[64]{0:T(128)}, f32[64]{0:T(128)S(1)}, u32[]{:S(2)}) copy-start(f32[64]{0:T(128)S(1)} %get-tuple-element.159) | copy-start | bytes 772
  25.5 64.8 %copy-start.68 = (f32[64]{0:T(128)}, f32[64]{0:T(128)S(1)}, u32[]{:S(2)}) copy-start(f32[64]{0:T(128)S(1)} %get-tuple-element.160) | copy-start | bytes 772
  25.5 64.8 %copy-start.70 = (f32[64]{0:T(128)}, f32[64]{0:T(128)S(1)}, u32[]{:S(2)}) copy-start(f32[64]{0:T(128)S(1)} %get-tuple-element.161) | copy-start | bytes 772
  25.5 64.8 %copy-start.72 = (f32[64]{0:T(128)}, f32[64]{0:T(128)S(1)}, u32[]{:S(2)}) copy-start(f32[64]{0:T(128)S(1)} %get-tuple-element.162) | copy-start | bytes 772
  25.5 64.8 %copy-start.74 = (f32[64]{0:T(128)}, f32[64]{0:T(128)S(1)}, u32[]{:S(2)}) copy-start(f32[64]{0:T(128)S(1)} %get-tuple-element.163) | copy-start | bytes 772
  26.8 82.9 %copy-start.18 = (f32[2048]{0:T(1024)}, f32[2048]{0:T(1024)S(1)}, u32[]{:S(2)}) copy-start(f32[2048]{0:T(1024)S(1)} %get-tuple-element.201) | copy-start | bytes 24580
  27.0 62.2 %collective-permute-start.3 = (bf16[1,64,3,134]{1,2,3,0:T(4,128)(2,1)S(1)}, bf16[1,64,3,134]{1,2,3,0:T(4,128)(2,1)S(1)}, u32[]{:S(2)}, u32[]{:S(2)}) collective-permute-start(bf16[1,64,3,134]{1,2,3,0:T(4,128)(2,1)S(1)} %get-tuple-element.144), channel_id=1, source_target_pairs={{1,0},{2,1},{3,2},{4,3},{5,4},{6,5},{7,6},{8,7},{9,8},{10,9},{11,1... | collective-permute-start | bytes 154376 | tf_op jit(solution)/shard_map/ppermute | solution.py:18
  33.5 56.1 %collective-permute-start.2 = (bf16[1,64,3,134]{1,2,3,0:T(4,128)(2,1)S(1)}, bf16[1,64,3,134]{1,2,3,0:T(4,128)(2,1)S(1)}, u32[]{:S(2)}, u32[]{:S(2)}) collective-permute-start(bf16[1,64,3,134]{1,2,3,0:T(4,128)(2,1)S(1)} %get-tuple-element.143), channel_id=1, source_target_pairs={{0,1},{1,2},{2,3},{3,4},{4,5},{5,6},{6,7},{7,8},{8,9},{9,10},{10,1... | collective-permute-start | bytes 154376 | tf_op jit(solution)/shard_map/ppermute | solution.py:16
  120.2 6.9 %collective-permute-start.4 = (bf16[1,64,16,3]{3,1,2,0:T(8,128)(2,1)S(1)}, bf16[1,64,16,3]{3,1,2,0:T(8,128)(2,1)S(1)}, u32[]{:S(2)}, u32[]{:S(2)}) collective-permute-start(bf16[1,64,16,3]{3,1,2,0:T(8,128)(2,1)S(1)} %get-tuple-element.149), channel_id=1, source_target_pairs={{0,16},{16,32},{32,48},{48,64},{64,80},{80,96},{96,112},{112,128},... | collective-permute-start | bytes 18440 | tf_op jit(solution)/shard_map/ppermute | solution.py:16
  123.3 15.1 %copy-start.5 = (f32[1,64,16,128]{3,2,1,0:T(8,128)S(1)}, f32[1,64,16,128]{3,2,1,0:T(8,128)}, u32[]{:S(2)}) copy-start(f32[1,64,16,128]{3,2,1,0:T(8,128)} %copy.108) | copy-start | bytes 1572868
  123.3 15.1 %copy-start.7 = (bf16[256,2048]{0,1:T(8,128)(2,1)S(1)}, bf16[256,2048]{0,1:T(8,128)(2,1)}, u32[]{:S(2)}) copy-start(bf16[256,2048]{0,1:T(8,128)(2,1)} %get-tuple-element.205) | copy-start | bytes 3145732
  123.4 15.1 %copy-start.15 = (f32[1,64,16,128]{3,2,1,0:T(8,128)S(1)}, f32[1,64,16,128]{3,2,1,0:T(8,128)}, u32[]{:S(2)}) copy-start(f32[1,64,16,128]{3,2,1,0:T(8,128)} %copy.95) | copy-start | bytes 1572868
  123.4 15.1 %copy-start.19 = (f32[2048]{0:T(1024)S(1)}, f32[2048]{0:T(1024)}, u32[]{:S(2)}) copy-start(f32[2048]{0:T(1024)} %copy-done.18) | copy-start | bytes 24580
  123.4 15.1 %copy-start.22 = (bf16[64,256]{1,0:T(8,128)(2,1)S(1)}, bf16[64,256]{1,0:T(8,128)(2,1)}, u32[]{:S(2)}) copy-start(bf16[64,256]{1,0:T(8,128)(2,1)} %param.22) | copy-start | bytes 98308
  123.4 15.1 %copy-start.87 = (f32[64]{0:T(128)S(1)}, f32[64]{0:T(128)}, u32[]{:S(2)}) copy-start(f32[64]{0:T(128)} %convert_element_type.420) | copy-start | bytes 772
  123.4 11.0 %collective-permute-start.5 = (bf16[1,64,16,3]{3,1,2,0:T(8,128)(2,1)S(1)}, bf16[1,64,16,3]{3,1,2,0:T(8,128)(2,1)S(1)}, u32[]{:S(2)}, u32[]{:S(2)}) collective-permute-start(bf16[1,64,16,3]{3,1,2,0:T(8,128)(2,1)S(1)} %get-tuple-element.150), channel_id=1, source_target_pairs={{16,0},{32,16},{48,32},{64,48},{80,64},{96,80},{112,96},{128,112},... | collective-permute-start | bytes 18440 | tf_op jit(solution)/shard_map/ppermute | solution.py:18
  135.2 10.0 %collective-permute-start.6 = (bf16[1,64,3,134]{3,1,2,0:T(8,128)(2,1)}, bf16[1,64,3,134]{3,1,2,0:T(8,128)(2,1)}, u32[]{:S(2)}, u32[]{:S(2)}) collective-permute-start(bf16[1,64,3,134]{3,1,2,0:T(8,128)(2,1)} %get-tuple-element.140), channel_id=1, source_target_pairs={{0,1},{1,2},{2,3},{3,4},{4,5},{5,6},{6,7},{7,8},{8,9},{9,10},{10,1... | collective-permute-start | bytes 154376 | tf_op jit(solution)/shard_map/ppermute | solution.py:16
  137.2 8.1 %collective-permute-start.7 = (bf16[1,64,3,134]{3,1,2,0:T(8,128)(2,1)}, bf16[1,64,3,134]{3,1,2,0:T(8,128)(2,1)}, u32[]{:S(2)}, u32[]{:S(2)}) collective-permute-start(bf16[1,64,3,134]{3,1,2,0:T(8,128)(2,1)} %get-tuple-element.139), channel_id=1, source_target_pairs={{1,0},{2,1},{3,2},{4,3},{5,4},{6,5},{7,6},{8,7},{9,8},{10,9},{11,1... | collective-permute-start | bytes 154376 | tf_op jit(solution)/shard_map/ppermute | solution.py:18
  156.9 331.4 %all-reduce.5.cloned.1.call-start = ((), (), s32[]{:S(2)}) async-start(), calls=%async_computation.2 | async-start | bytes 262144 | tf_op jit(solution)/shard_map/psum | solution.py:179
  (64 other events, 408.6 us)
Sparse Core Ops, SparseCore 0:
  11.7 68.0 all-gather.2
  157.0 65.3 all-gather.4
  228.2 260.0 all-reduce.4
where the time goes:
time: 499 us; the launch traced here: 498 us
  waiting for transfers between devices  244 us (49%)
  blocking collectives  107 us (21%)
  local copies, waits for them, and re-layouts  46.1 us (9%)
  other arithmetic  45.4 us (9%)
  starting transfers between devices  24.7 us (5%)
  between operations  15.4 us (3%)
  matrix products  15.1 us (3%)
    psum x1, waiting for transfers between devices, shards(): lax.psum((g_depth, gain_gradient, g_bias, g_up_w, g_up_b, g_down, g_scale...  195 us
    psum x1, blocking collectives, shards(): lax.psum((g_depth, gain_gradient, g_bias, g_up_w, g_up_b, g_down, g_scale...  107 us
    all_gather x1, waiting for transfers between devices, shards(): lax.all_gather(upper, 'lon', axis=3, tiled=True)  42.1 us
    ppermute x4, starting transfers between devices, extended_2(): lax.ppermute(tail, axis, [(i, (i + 1) % count) for i in range(ends)])  16.4 us
    reduce_sum x4, other arithmetic, shards(): jnp.sum(d_conv_f * extended[:, :, row_tap:row_tap + rows, col_tap:col_tap...  10.9 us
    reduce_sum x1, other arithmetic, cell_terms(): mean_c = jnp.mean(conv, axis=0, keepdims=True)  9.98 us
  transfers between devices with their start and end apart: 11, of which 3 were waited for; matrix products, arithmetic and copies ran while one was open for 12% of the time, Pallas kernels for 0%

commit v1 on v0

--- a/solution.py
+++ b/solution.py
@@ -177,7 +177,7 @@
     grad_fields = (mask_f[None, None] * cotangent.astype(jnp.float32) + own).astype(jnp.bfloat16)
     gain_gradient, g_bias, g_up_w, g_up_b, g_down, g_scale = parts
     summed = lax.psum(
-        (g_depth, gain_gradient, g_bias, g_up_w, g_up_b, g_down, g_scale), ("lon", "lat")
+        lax.psum((g_depth, gain_gradient, g_bias, g_up_w, g_up_b, g_down, g_scale), "lat"), "lon"
     )
     return (
         output,

time: 499 us -> 643 us (1.29)
  blocking collectives: 107 us -> 199 us
  waiting for transfers between devices: 244 us -> 304 us
  local copies, waits for them, and re-layouts: 46.1 us -> 39 us
    psum x0 -> x1, waiting for transfers between devices: none -> 250 us  [shards(): lax.psum(lax.psum((g_depth, gain_gradient, g_bias, g_up_w, g_up_b, g_down...]
    psum x1, waiting for transfers between devices: 195 us -> 0.01 us  [shards(): lax.psum((g_depth, gain_gradient, g_bias, g_up_w, g_up_b, g_down, g_scale...]
    psum x0 -> x1, blocking collectives: none -> 149 us  [shards(): lax.psum(lax.psum((g_depth, gain_gradient, g_bias, g_up_w, g_up_b, g_down...]
    psum x1, blocking collectives: 107 us -> 50.3 us  [shards(): lax.psum((g_depth, gain_gradient, g_bias, g_up_w, g_up_b, g_down, g_scale...]
  transfers between devices with their start and end apart: 11 -> 12, of which waited for: 3 -> 5; matrix products, arithmetic and copies ran while one was open for 12% -> 9% of each run, Pallas kernels for 0% -> 0%
where the time goes in v1:
time: 643 us; the launch traced here: 642 us
  waiting for transfers between devices  304 us (47%)
  blocking collectives  199 us (31%)
  other arithmetic  44.5 us (7%)
  local copies, waits for them, and re-layouts  39 us (6%)
  starting transfers between devices  24.9 us (4%)
  matrix products  15.7 us (2%)
  between operations  15.4 us (2%)
    psum x1, waiting for transfers between devices, shards(): lax.psum(lax.psum((g_depth, gain_gradient, g_bias, g_up_w, g_up_b, g_down...  250 us
    psum x1, blocking collectives, shards(): lax.psum(lax.psum((g_depth, gain_gradient, g_bias, g_up_w, g_up_b, g_down...  149 us
    psum x1, blocking collectives, shards(): lax.psum((g_depth, gain_gradient, g_bias, g_up_w, g_up_b, g_down, g_scale...  50.3 us
    all_gather x1, waiting for transfers between devices, shards(): lax.all_gather(upper, 'lon', axis=3, tiled=True)  42.4 us
    ppermute x4, starting transfers between devices, extended_2(): lax.ppermute(tail, axis, [(i, (i + 1) % count) for i in range(ends)])  16.7 us
  transfers between devices with their start and end apart: 12, of which 5 were waited for; matrix products, arithmetic and copies ran while one was open for 9% of the time, Pallas kernels for 0%

profile of v1, /device:TPU:1, one launch (start us, length us, event | category | flops | bytes accessed | tf_op | source)
XLA Modules:
  0.0 642.2 jit_solution(14889142366612477725)
XLA Ops:
  7.3 1.0 slice.730
  9.0 1.5 copy.94
  10.5 7.2 %collective-permute-start = (bf16[1,64,16,3]{1,2,3,0:T(8,128)(2,1)S(1)}, bf16[1,64,16,3]{1,2,3,0:T(8,128)(2,1)S(1)}, u32[]{:S(2)}, u32[]{:S(2)}) collective-permute-start(bf16[1,64,16,3]{1,2,3,0:T(8,128)(2,1)S(1)} %get-tuple-element.154), channel_id=1, source_target_pairs={{0,16},{16,32},{32,48},{48,64},{64,80},{80,96},{96,112},{112,128},... | collective-permute-start | bytes 18440 | tf_op jit(solution)/shard_map/ppermute | solution.py:16
  17.7 3.5 collective-permute-start.1
  21.3 0.7 convert_element_type.421
  22.0 2.0 gather_fusion
  26.6 1.3 collective-permute-start.3
  28.5 1.4 copy.95
  30.9 1.1 copy.108
  32.5 4.2 collective-permute-start.2
  36.7 42.4 %all-gather.3.cloned.1.call-done = bf16[1,64,3,4096]{3,1,2,0:T(8,128)(2,1)} async-done(((bf16[1,64,3,128]{3,1,2,0:T(8,128)(2,1)}), bf16[1,64,3,4096]{3,1,2,0:T(8,128)(2,1)}) %all-gather.3.cloned.1.call-update) | async-done | bytes 1572880 | tf_op jit(solution)/shard_map/all_gather | solution.py:116
  79.1 6.4 copy.102
  85.5 3.0 gather_fusion.1
  89.7 10.5 %fusion.134 = (f32[16,128]{0,1:T(8,128)S(1)}, f32[1,64,16,128]{1,2,3,0:T(8,128)S(1)}) fusion(bf16[1,64,19,134]{1,2,3,0:T(8,128)(2,1)S(1)} %get-tuple-element.149, f32[64]{0:T(128)S(1)} %get-tuple-element.159, f32[64]{0:T(128)S(1)} %get-tuple-element.160, f32[64]{0:T(128)S(1)} %get-tuple-element.161, f32[64]{0:T(128)S(1)} %get-tuple-element.162, ...), kind=kLoop, calls=%fused_computation.375 | loop fusion | flops 20051968 | bytes 11829504 | tf_op jit(solution)/shard_map/reduce_sum | solution.py:33
  100.2 1.4 copy.103
  102.5 6.9 %fusion.5 = (bf16[256,2048]{0,1:T(8,128)(2,1)}, f32[256,2048]{0,1:T(8,128)S(1)}) fusion(f32[256]{0:T(256)S(1)} %convert_element_type.474, bf16[256,64]{0,1:T(8,128)(2,1)S(1)} %copy-done, f32[64]{0:T(128)} %convert_element_type.472, f32[64]{0:T(128)} %convert_element_type.471, f32[2048]{0:T(1024)S(1)} %rsqrt_bitcast_fusion, ...), kind=kOutput, calls=%fused_computation.63 | convolution fusion | flops 102367232 | bytes 3720704 | tf_op jit(solution)/shard_map/dot_general | solution.py:43
  109.5 2.0 convert_reduce_fusion
  111.5 1.8 fusion.121
  113.4 0.9 fusion.123
  115.6 1.0 copy.109
  116.6 4.4 fusion.113
  121.2 3.3 collective-permute-start.4
  124.5 1.9 collective-permute-start.5
  126.4 1.7 fusion.133
  128.2 7.2 %collective-permute-done.5 = bf16[1,64,16,3]{3,1,2,0:T(8,128)(2,1)S(1)} collective-permute-done((bf16[1,64,16,3]{3,1,2,0:T(8,128)(2,1)S(1)}, bf16[1,64,16,3]{3,1,2,0:T(8,128)(2,1)S(1)}, u32[]{:S(2)}, u32[]{:S(2)}) %collective-permute-start.5) | collective-permute-done | bytes 6176 | tf_op jit(solution)/shard_map/ppermute | solution.py:18
  135.3 0.8 pad_maximum_fusion.8
  136.2 2.1 collective-permute-start.6
  138.2 1.3 collective-permute-start.7
  139.6 1.0 fusion.132
  140.7 4.2 collective-permute-done.7
  144.8 1.4 pad_maximum_fusion.1
  146.3 1.4 pad_maximum_fusion.2
  147.8 7.0 %multiply_add_fusion = f32[1,64,19,128]{3,1,2,0:T(8,128)S(1)} fusion(bf16[1,64,19,134]{3,1,2,0:T(8,128)(2,1)S(1)} %get-tuple-element.145, bf16[1,64,22,134]{3,1,2,0:T(8,128)(2,1)S(1)} %pad_maximum_fusion.1, bf16[1,64,19,134]{3,1,2,0:T(8,128)(2,1)S(1)} %get-tuple-element.144, f32[64]{0:T(128)} %copy-done.38, f32[64]{0:T(128)} %copy-done.39, ...), kind=kLoop, calls=%fused_computation.239 | loop fusion | flops 22724608 | bytes 10072832 | tf_op jit(solution)/shard_map/add | solution.py:164
  154.8 0.9 copy-done.9
  156.3 2.2 multiply_reduce_fusion.1
  158.9 0.7 copy.119
  159.6 1.0 fusion.112
  160.9 1.2 fusion.92
  162.2 3.3 fusion.85
  165.7 50.3 %all-reduce.3 = (f32[64,7,7]{0,2,1:T(8,128)S(1)}, f32[64]{0:T(128)S(1)}, f32[64]{0:T(128)S(1)}, f32[256]{0:T(256)S(1)}, f32[64]{0:T(128)S(1)}) all-reduce(f32[64,7,7]{0,2,1:T(8,128)S(1)} %constant_dynamic-update-slice_fusion, f32[64]{0:T(128)S(1)} %copy-done.87, f32[64]{0:T(128)S(1)} %reduce_sum.567, ...), channel_id=1, replica_groups=mesh['lon'=32,'lat'=16] {'lat'}, use_global_device_ids=true, to_apply=%region_53.54 | all-reduce | flops 3584 | bytes 28672 | tf_op jit(solution)/shard_map/psum | solution.py:180
  216.0 148.8 %all-reduce.1 = (f32[64,7,7]{0,2,1:T(8,128)}, f32[64]{0:T(128)}, f32[64]{0:T(128)}, f32[256]{0:T(256)}, f32[64]{0:T(128)}) all-reduce(f32[64,7,7]{0,2,1:T(8,128)S(1)} %get-tuple-element.131, f32[64]{0:T(128)S(1)} %get-tuple-element.132, f32[64]{0:T(128)S(1)} %get-tuple-element.133, ...), channel_id=1, replica_groups=mesh['lon'=32,'lat'=16] {'lon'}, use_global_device_ids=true, to_apply=%region_54.55 | all-reduce | flops 3584 | bytes 28672 | tf_op jit(solution)/shard_map/psum | solution.py:179
  364.8 6.4 copy.112
  371.3 6.2 bitcast_convert_fusion
  377.5 4.3 gather_fusion.2
  382.1 0.9 copy.115
  383.0 249.8 %all-reduce.8.cloned.1.call-done = (f32[256,64]{0,1:T(8,128)}, f32[64,256]{1,0:T(8,128)}) async-done(((f32[256,64]{0,1:T(8,128)}, f32[64,256]{1,0:T(8,128)}), (f32[256,64]{0,1:T(8,128)}, f32[64,256]{1,0:T(8,128)})) %all-reduce.8.cloned.1.call-update) | async-done | bytes 131088 | tf_op jit(solution)/shard_map/psum | solution.py:179
  632.8 1.5 copy.161
  634.2 1.5 copy.162
  (256 shorter events, 10.0 us)
Async XLA Ops:
  7.2 95.3 %copy-start = (bf16[256,64]{0,1:T(8,128)(2,1)S(1)}, bf16[256,64]{0,1:T(8,128)(2,1)}, u32[]{:S(2)}) copy-start(bf16[256,64]{0,1:T(8,128)(2,1)} %param.20) | copy-start | bytes 98308
  7.2 71.9 %all-gather.3.cloned.1.call-start = ((), (), s32[]{:S(2)}) async-start(), calls=%async_computation | async-start | bytes 1622016 | tf_op jit(solution)/shard_map/all_gather | solution.py:116
  8.9 355.9 %all-reduce.10.cloned.1.call-start = ((), (), s32[]{:S(2)}) async-start(), calls=%async_computation.3 | async-start | bytes 262144 | tf_op jit(solution)/shard_map/psum | solution.py:180
  10.5 15.9 %collective-permute-start = (bf16[1,64,16,3]{1,2,3,0:T(8,128)(2,1)S(1)}, bf16[1,64,16,3]{1,2,3,0:T(8,128)(2,1)S(1)}, u32[]{:S(2)}, u32[]{:S(2)}) collective-permute-start(bf16[1,64,16,3]{1,2,3,0:T(8,128)(2,1)S(1)} %get-tuple-element.154), channel_id=1, source_target_pairs={{0,16},{16,32},{32,48},{48,64},{64,80},{80,96},{96,112},{112,128},... | collective-permute-start | bytes 18440 | tf_op jit(solution)/shard_map/ppermute | solution.py:16
  17.7 8.7 %collective-permute-start.1 = (bf16[1,64,16,3]{1,2,3,0:T(8,128)(2,1)S(1)}, bf16[1,64,16,3]{1,2,3,0:T(8,128)(2,1)S(1)}, u32[]{:S(2)}, u32[]{:S(2)}) collective-permute-start(bf16[1,64,16,3]{1,2,3,0:T(8,128)(2,1)S(1)} %get-tuple-element.155), channel_id=1, source_target_pairs={{16,0},{32,16},{48,32},{64,48},{80,64},{96,80},{112,96},{128,112},... | collective-permute-start | bytes 18440 | tf_op jit(solution)/shard_map/ppermute | solution.py:18
  24.7 64.6 %copy-start.24 = (f32[64]{0:T(128)}, f32[64]{0:T(128)S(1)}, u32[]{:S(2)}) copy-start(f32[64]{0:T(128)S(1)} %get-tuple-element.196) | copy-start | bytes 772
  24.7 64.6 %copy-start.26 = (f32[64]{0:T(128)}, f32[64]{0:T(128)S(1)}, u32[]{:S(2)}) copy-start(f32[64]{0:T(128)S(1)} %get-tuple-element.197) | copy-start | bytes 772
  24.7 64.6 %copy-start.28 = (f32[64]{0:T(128)}, f32[64]{0:T(128)S(1)}, u32[]{:S(2)}) copy-start(f32[64]{0:T(128)S(1)} %get-tuple-element.198) | copy-start | bytes 772
  24.7 64.6 %copy-start.29 = (f32[64]{0:T(128)}, f32[64]{0:T(128)S(1)}, u32[]{:S(2)}) copy-start(f32[64]{0:T(128)S(1)} %get-tuple-element.199) | copy-start | bytes 772
  24.7 64.6 %copy-start.30 = (f32[64]{0:T(128)}, f32[64]{0:T(128)S(1)}, u32[]{:S(2)}) copy-start(f32[64]{0:T(128)S(1)} %get-tuple-element.200) | copy-start | bytes 772
  24.7 64.6 %copy-start.31 = (f32[64]{0:T(128)}, f32[64]{0:T(128)S(1)}, u32[]{:S(2)}) copy-start(f32[64]{0:T(128)S(1)} %get-tuple-element.201) | copy-start | bytes 772
  24.8 64.6 %copy-start.32 = (f32[64]{0:T(128)}, f32[64]{0:T(128)S(1)}, u32[]{:S(2)}) copy-start(f32[64]{0:T(128)S(1)} %get-tuple-element.202) | copy-start | bytes 772
  24.8 64.6 %copy-start.33 = (f32[64]{0:T(128)}, f32[64]{0:T(128)S(1)}, u32[]{:S(2)}) copy-start(f32[64]{0:T(128)S(1)} %get-tuple-element.203) | copy-start | bytes 772
  24.8 64.6 %copy-start.34 = (f32[64]{0:T(128)}, f32[64]{0:T(128)S(1)}, u32[]{:S(2)}) copy-start(f32[64]{0:T(128)S(1)} %get-tuple-element.204) | copy-start | bytes 772
  24.8 64.6 %copy-start.35 = (f32[64]{0:T(128)}, f32[64]{0:T(128)S(1)}, u32[]{:S(2)}) copy-start(f32[64]{0:T(128)S(1)} %get-tuple-element.205) | copy-start | bytes 772
  24.8 64.6 %copy-start.36 = (f32[64]{0:T(128)}, f32[64]{0:T(128)S(1)}, u32[]{:S(2)}) copy-start(f32[64]{0:T(128)S(1)} %get-tuple-element.206) | copy-start | bytes 772
  24.8 64.6 %copy-start.37 = (f32[64]{0:T(128)}, f32[64]{0:T(128)S(1)}, u32[]{:S(2)}) copy-start(f32[64]{0:T(128)S(1)} %get-tuple-element.158) | copy-start | bytes 772
  24.8 64.6 %copy-start.38 = (f32[64]{0:T(128)}, f32[64]{0:T(128)S(1)}, u32[]{:S(2)}) copy-start(f32[64]{0:T(128)S(1)} %get-tuple-element.159) | copy-start | bytes 772
  24.8 64.6 %copy-start.39 = (f32[64]{0:T(128)}, f32[64]{0:T(128)S(1)}, u32[]{:S(2)}) copy-start(f32[64]{0:T(128)S(1)} %get-tuple-element.160) | copy-start | bytes 772
  24.9 64.6 %copy-start.40 = (f32[64]{0:T(128)}, f32[64]{0:T(128)S(1)}, u32[]{:S(2)}) copy-start(f32[64]{0:T(128)S(1)} %get-tuple-element.161) | copy-start | bytes 772
  24.9 64.6 %copy-start.41 = (f32[64]{0:T(128)}, f32[64]{0:T(128)S(1)}, u32[]{:S(2)}) copy-start(f32[64]{0:T(128)S(1)} %get-tuple-element.162) | copy-start | bytes 772
  24.9 64.6 %copy-start.42 = (f32[64]{0:T(128)}, f32[64]{0:T(128)S(1)}, u32[]{:S(2)}) copy-start(f32[64]{0:T(128)S(1)} %get-tuple-element.163) | copy-start | bytes 772
  24.9 64.6 %copy-start.43 = (f32[64]{0:T(128)}, f32[64]{0:T(128)S(1)}, u32[]{:S(2)}) copy-start(f32[64]{0:T(128)S(1)} %get-tuple-element.164) | copy-start | bytes 772
  24.9 64.6 %copy-start.44 = (f32[64]{0:T(128)}, f32[64]{0:T(128)S(1)}, u32[]{:S(2)}) copy-start(f32[64]{0:T(128)S(1)} %get-tuple-element.165) | copy-start | bytes 772
  24.9 64.6 %copy-start.45 = (f32[64]{0:T(128)}, f32[64]{0:T(128)S(1)}, u32[]{:S(2)}) copy-start(f32[64]{0:T(128)S(1)} %get-tuple-element.166) | copy-start | bytes 772
  24.9 64.6 %copy-start.46 = (f32[64]{0:T(128)}, f32[64]{0:T(128)S(1)}, u32[]{:S(2)}) copy-start(f32[64]{0:T(128)S(1)} %get-tuple-element.167) | copy-start | bytes 772
  24.9 64.6 %copy-start.47 = (f32[64]{0:T(128)}, f32[64]{0:T(128)S(1)}, u32[]{:S(2)}) copy-start(f32[64]{0:T(128)S(1)} %get-tuple-element.168) | copy-start | bytes 772
  24.9 64.6 %copy-start.48 = (f32[64]{0:T(128)}, f32[64]{0:T(128)S(1)}, u32[]{:S(2)}) copy-start(f32[64]{0:T(128)S(1)} %get-tuple-element.169) | copy-start | bytes 772
  24.9 64.6 %copy-start.49 = (f32[64]{0:T(128)}, f32[64]{0:T(128)S(1)}, u32[]{:S(2)}) copy-start(f32[64]{0:T(128)S(1)} %get-tuple-element.170) | copy-start | bytes 772
  25.0 64.6 %copy-start.50 = (f32[64]{0:T(128)}, f32[64]{0:T(128)S(1)}, u32[]{:S(2)}) copy-start(f32[64]{0:T(128)S(1)} %get-tuple-element.171) | copy-start | bytes 772
  25.0 64.6 %copy-start.51 = (f32[64]{0:T(128)}, f32[64]{0:T(128)S(1)}, u32[]{:S(2)}) copy-start(f32[64]{0:T(128)S(1)} %get-tuple-element.172) | copy-start | bytes 772
  25.0 64.6 %copy-start.52 = (f32[64]{0:T(128)}, f32[64]{0:T(128)S(1)}, u32[]{:S(2)}) copy-start(f32[64]{0:T(128)S(1)} %get-tuple-element.173) | copy-start | bytes 772
  25.0 64.6 %copy-start.53 = (f32[64]{0:T(128)}, f32[64]{0:T(128)S(1)}, u32[]{:S(2)}) copy-start(f32[64]{0:T(128)S(1)} %get-tuple-element.174) | copy-start | bytes 772
  25.0 64.6 %copy-start.54 = (f32[64]{0:T(128)}, f32[64]{0:T(128)S(1)}, u32[]{:S(2)}) copy-start(f32[64]{0:T(128)S(1)} %get-tuple-element.175) | copy-start | bytes 772
  25.0 64.6 %copy-start.55 = (f32[64]{0:T(128)}, f32[64]{0:T(128)S(1)}, u32[]{:S(2)}) copy-start(f32[64]{0:T(128)S(1)} %get-tuple-element.176) | copy-start | bytes 772
  25.6 64.0 %copy-start.56 = (f32[64]{0:T(128)}, f32[64]{0:T(128)S(1)}, u32[]{:S(2)}) copy-start(f32[64]{0:T(128)S(1)} %get-tuple-element.177) | copy-start | bytes 772
  25.7 64.0 %copy-start.57 = (f32[64]{0:T(128)}, f32[64]{0:T(128)S(1)}, u32[]{:S(2)}) copy-start(f32[64]{0:T(128)S(1)} %get-tuple-element.178) | copy-start | bytes 772
  25.7 64.0 %copy-start.58 = (f32[64]{0:T(128)}, f32[64]{0:T(128)S(1)}, u32[]{:S(2)}) copy-start(f32[64]{0:T(128)S(1)} %get-tuple-element.179) | copy-start | bytes 772
  25.7 64.0 %copy-start.59 = (f32[64]{0:T(128)}, f32[64]{0:T(128)S(1)}, u32[]{:S(2)}) copy-start(f32[64]{0:T(128)S(1)} %get-tuple-element.180) | copy-start | bytes 772
  25.7 64.0 %copy-start.60 = (f32[64]{0:T(128)}, f32[64]{0:T(128)S(1)}, u32[]{:S(2)}) copy-start(f32[64]{0:T(128)S(1)} %get-tuple-element.181) | copy-start | bytes 772
  26.6 61.8 %collective-permute-start.3 = (bf16[1,64,3,134]{1,2,3,0:T(4,128)(2,1)S(1)}, bf16[1,64,3,134]{1,2,3,0:T(4,128)(2,1)S(1)}, u32[]{:S(2)}, u32[]{:S(2)}) collective-permute-start(bf16[1,64,3,134]{1,2,3,0:T(4,128)(2,1)S(1)} %get-tuple-element.151), channel_id=1, source_target_pairs={{1,0},{2,1},{3,2},{4,3},{5,4},{6,5},{7,6},{8,7},{9,8},{10,9},{11,1... | collective-permute-start | bytes 154376 | tf_op jit(solution)/shard_map/ppermute | solution.py:18
  32.5 56.3 %collective-permute-start.2 = (bf16[1,64,3,134]{1,2,3,0:T(4,128)(2,1)S(1)}, bf16[1,64,3,134]{1,2,3,0:T(4,128)(2,1)S(1)}, u32[]{:S(2)}, u32[]{:S(2)}) collective-permute-start(bf16[1,64,3,134]{1,2,3,0:T(4,128)(2,1)S(1)} %get-tuple-element.150), channel_id=1, source_target_pairs={{0,1},{1,2},{2,3},{3,4},{4,5},{5,6},{6,7},{7,8},{8,9},{9,10},{10,1... | collective-permute-start | bytes 154376 | tf_op jit(solution)/shard_map/ppermute | solution.py:16
  121.2 7.0 %collective-permute-start.4 = (bf16[1,64,16,3]{3,1,2,0:T(8,128)(2,1)S(1)}, bf16[1,64,16,3]{3,1,2,0:T(8,128)(2,1)S(1)}, u32[]{:S(2)}, u32[]{:S(2)}) collective-permute-start(bf16[1,64,16,3]{3,1,2,0:T(8,128)(2,1)S(1)} %get-tuple-element.156), channel_id=1, source_target_pairs={{0,16},{16,32},{32,48},{48,64},{64,80},{80,96},{96,112},{112,128},... | collective-permute-start | bytes 18440 | tf_op jit(solution)/shard_map/ppermute | solution.py:16
  124.5 10.9 %collective-permute-start.5 = (bf16[1,64,16,3]{3,1,2,0:T(8,128)(2,1)S(1)}, bf16[1,64,16,3]{3,1,2,0:T(8,128)(2,1)S(1)}, u32[]{:S(2)}, u32[]{:S(2)}) collective-permute-start(bf16[1,64,16,3]{3,1,2,0:T(8,128)(2,1)S(1)} %get-tuple-element.157), channel_id=1, source_target_pairs={{16,0},{32,16},{48,32},{64,48},{80,64},{96,80},{112,96},{128,112},... | collective-permute-start | bytes 18440 | tf_op jit(solution)/shard_map/ppermute | solution.py:18
  136.2 4.5 collective-permute-start.6
  138.2 6.6 %collective-permute-start.7 = (bf16[1,64,3,134]{3,1,2,0:T(8,128)(2,1)}, bf16[1,64,3,134]{3,1,2,0:T(8,128)(2,1)}, u32[]{:S(2)}, u32[]{:S(2)}) collective-permute-start(bf16[1,64,3,134]{3,1,2,0:T(8,128)(2,1)} %get-tuple-element.146), channel_id=1, source_target_pairs={{1,0},{2,1},{3,2},{4,3},{5,4},{6,5},{7,6},{8,7},{9,8},{10,9},{11,1... | collective-permute-start | bytes 154376 | tf_op jit(solution)/shard_map/ppermute | solution.py:18
  140.6 224.2 %all-gather.5.cloned.1.call-start = ((), (), s32[]{:S(2)}) async-start(), calls=%async_computation.1 | async-start | bytes 1622016 | tf_op jit(solution)/shard_map/all_gather | solution.py:173
  156.3 476.5 %all-reduce.8.cloned.1.call-start = ((), (), s32[]{:S(2)}) async-start(), calls=%async_computation.2 | async-start | bytes 262144 | tf_op jit(solution)/shard_map/psum | solution.py:179
  (58 other events, 641.5 us)
Sparse Core Ops, SparseCore 0:
  11.7 67.3 all-gather.2
  140.7 135.3 all-reduce.9
  280.2 70.2 all-gather.4
  364.9 267.7 all-reduce.7
